TPU v7x, 256 devices: a whole 4x4x8 slice. The times are simulated.
256 devices in a mesh: gx: 16 (over y, x), gy: 16 (over z, core).
Axes of the slice: x: 4, y: 4, z: 8, core: 2. Of those that a mesh axis runs over, the one named last changes fastest.
Arguments:
- vectors: float32 [8, 128, 256, 256], P(None, 'gx', 'gy'), may hold values from -10 to 10
- weight_x: float32 [128, 256, 256], P('gx', 'gy'), may hold values from 0.05 to 1
- weight_y: float32 [128, 256, 256], P('gx', 'gy'), may hold values from 0.05 to 1
- weight_z: float32 [128, 256, 256], P('gx', 'gy'), may hold values from 0.05 to 1
Outputs:
- refined: float32 [8, 128, 256, 256], P(None, 'gx', 'gy')
- eigenvalues: float32 [8], replicated
All inputs are finite; a program needn't handle non-finite values.
Results may differ from a plain program's by a relative error of at most 0.000075.
Values sent between devices are 32-bit elements; how exact they have to be, the bound alone decides.
No kernel may reach another device: no remote copies, remote signals or barrier semaphores. Data moves between devices by JAX's collectives and lax.ppermute only.
A program may use at most 128 MiB of HBM per device.

v0:
```python
import jax
import jax.numpy as jnp
from jax import lax
from jax.sharding import PartitionSpec as P

COARSE_SWEEPS = 4
OMEGA = 0.8
SHIFT = 0.1


def shifted(shard, axis, by):
    count = lax.axis_size(axis)
    pairs = [(i, i + by) for i in range(count) if 0 <= i + by < count]
    return lax.ppermute(shard, axis, pairs)


def with_halo(cells, sides, width):
    for axis, dim in sides:
        count = lax.axis_size(axis)
        ends = count - 1
        head = lax.slice_in_dim(cells, 0, width, axis=dim)
        tail = lax.slice_in_dim(cells, cells.shape[dim] - width, cells.shape[dim], axis=dim)
        cells = jnp.concatenate(
            [
                lax.ppermute(tail, axis, [(i, (i + 1) % count) for i in range(ends)]),
                cells,
                lax.ppermute(head, axis, [((i + 1) % count, i) for i in range(ends)]),
            ],
            axis=dim,
        )
    return cells


def lower_x(weights):
    rim = shifted(weights[-1:], "gx", 1)
    return jnp.concatenate([rim, weights[:-1]], 0)


def lower_y(weights):
    rim = shifted(weights[:, -1:], "gy", 1)
    return jnp.concatenate([rim, weights[:, :-1]], 1)


def lower_z(weights):
    return jnp.concatenate([jnp.zeros_like(weights[:, :, :1]), weights[:, :, :-1]], 2)


def trimmed(array):
    return array[..., 1:-1, 1:-1, :]


def inner_sum(field, parts):
    wx, lx, wy, ly, wz, lz = parts
    centre = trimmed(field)
    zpadded = jnp.pad(centre, ((0, 0), (0, 0), (0, 0), (1, 1)))
    total = wx[None] * field[:, 2:, 1:-1] + lx[None] * field[:, :-2, 1:-1]
    total = total + wy[None] * field[:, 1:-1, 2:] + ly[None] * field[:, 1:-1, :-2]
    total = total + wz[None] * zpadded[..., 2:] + lz[None] * zpadded[..., :-2]
    return total


def neighbours(field, parts, level):
    if level == "fine":
        padded = with_halo(field, (("gx", 1), ("gy", 2)), 1)
    else:
        padded = with_halo(field, (("gx", 1), ("gy", 2)), 1)
    return inner_sum(padded, parts)


def jacobi(guess, source, diag, parts, level):
    return (
        guess
        + OMEGA * (source - (diag[None] * guess - neighbours(guess, parts, level))) / diag[None]
    )


def rayleigh_sums(vectors, applied, degree):
    return lax.psum(
        (
            jnp.sum(vectors * applied, axis=(1, 2, 3)),
            jnp.sum(vectors * (degree[None] * vectors), axis=(1, 2, 3)),
        ),
        ("gx", "gy"),
    )


def coarse_weights(wx, wy, wz, degree):
    sx, sy, sz = wx.shape
    shape = (sx // 2, 2, sy // 2, 2, sz // 2, 2)
    cx = wx.reshape(shape)[:, 1].sum(axis=(2, 4))
    cy = wy.reshape(shape)[:, :, :, 1].sum(axis=(1, 4))
    cz = wz.reshape(shape)[..., 1].sum(axis=(1, 3))
    dsum = degree.reshape(shape).sum(axis=(1, 3, 5))
    return (cx, cy, cz, dsum)


def restrict(field):
    kk, sx, sy, sz = field.shape
    return field.reshape(kk, sx // 2, 2, sy // 2, 2, sz // 2, 2).sum(axis=(2, 4, 6))


def prolong(field):
    kk, sx, sy, sz = field.shape
    return jnp.broadcast_to(field[:, :, None, :, None, :, None], (kk, sx, 2, sy, 2, sz, 2)).reshape(
        kk, 2 * sx, 2 * sy, 2 * sz
    )


def per_device(vectors, weight_x, weight_y, weight_z):
    local_x, local_y, depth = weight_x.shape
    span_x = local_x * lax.axis_size("gx")
    span_y = local_y * lax.axis_size("gy")
    pos_x = lax.axis_index("gx") * local_x + lax.broadcasted_iota(jnp.int32, (local_x, 1, 1), 0)
    pos_y = lax.axis_index("gy") * local_y + lax.broadcasted_iota(jnp.int32, (1, local_y, 1), 1)
    pos_z = lax.broadcasted_iota(jnp.int32, (1, 1, depth), 2)
    wx = jnp.where(pos_x < span_x - 1, weight_x, jnp.zeros_like(weight_x))
    wy = jnp.where(pos_y < span_y - 1, weight_y, jnp.zeros_like(weight_y))
    wz = jnp.where(pos_z < depth - 1, weight_z, jnp.zeros_like(weight_z))
    parts = (wx, lower_x(wx), wy, lower_y(wy), wz, lower_z(wz))
    degree = parts[0] + parts[1] + parts[2] + parts[3] + parts[4] + parts[5]
    applied = degree[None] * vectors - neighbours(vectors, parts, "fine")
    numer, denom = rayleigh_sums(vectors, applied, degree)
    eigenvalues = numer / denom
    resid = applied - eigenvalues[:, None, None, None] * (degree[None] * vectors)
    dfine = (1.0 + SHIFT) * degree
    guess = OMEGA * resid / dfine[None]
    guess = jacobi(guess, resid, dfine, parts, "fine")
    fine_rest = resid - (dfine[None] * guess - neighbours(guess, parts, "fine"))
    cx, cy, cz, dsum = coarse_weights(wx, wy, wz, degree)
    cparts = (cx, lower_x(cx), cy, lower_y(cy), cz, lower_z(cz))
    dcoarse = cparts[0] + cparts[1] + cparts[2] + cparts[3] + cparts[4] + cparts[5] + SHIFT * dsum
    rcoarse = restrict(fine_rest)
    correction = OMEGA * rcoarse / dcoarse[None]
    for sweep in range(COARSE_SWEEPS - 1):
        correction = jacobi(correction, rcoarse, dcoarse, cparts, "coarse")
    guess = guess + prolong(correction)
    guess = jacobi(guess, resid, dfine, parts, "fine")
    updated = vectors - guess
    local_gram = jnp.einsum(
        "aijk,bijk->ab", updated, degree[None] * updated, precision=lax.Precision.HIGHEST
    )
    gram = lax.psum(local_gram, ("gx", "gy"))
    gram = gram / (span_x * span_y * depth)
    chol = jnp.linalg.cholesky(gram)
    flat = updated.reshape(updated.shape[0], -1)
    refined = jax.scipy.linalg.solve_triangular(chol, flat, lower=True).reshape(updated.shape)
    return (refined, eigenvalues)


def solution(mesh):
    return jax.shard_map(
        per_device,
        mesh=mesh,
        in_specs=(
            P(None, "gx", "gy", None),
            P("gx", "gy", None),
            P("gx", "gy", None),
            P("gx", "gy", None),
        ),
        out_specs=(P(None, "gx", "gy", None), P()),
        check_vma=False,
    )
```

profile of v0, /device:TPU:1, one launch (start us, length us, event | category | flops | bytes accessed | tf_op | source)
XLA Modules:
  0.0 427.5 jit_solution(8508537190117706973)
XLA Ops:
  1.7 3.9 collective-permute-start
  6.6 4.4 %collective-permute-start.1 = (f32[8,1,256]{2,1,0:T(1,128)S(1)}, f32[8,1,256]{2,1,0:T(1,128)S(1)}, u32[]{:S(2)}, u32[]{:S(2)}) collective-permute-start(f32[8,1,256]{2,1,0:T(1,128)S(1)} %slice.374), channel_id=1, source_target_pairs={{0,1},{1,2},{2,3},{3,4},{4,5},{5,6},{6,7},{7,8},{8,9},{9,10},{10,1... | collective-permute-start | bytes 24584 | tf_op jit(solution)/shard_map/ppermute | solution.py:14
  12.0 3.1 collective-permute-start.3
  16.5 9.8 %reshape.74 = f32[4,2,8,2,128,2]{5,4,3,2,1,0:T(8,128)} reshape(f32[8,16,256]{2,1,0:T(8,128)S(1)} %broadcast_select_fusion.2) | data formatting | bytes 262144 | tf_op jit(solution)/shard_map/reshape | solution.py:90
  28.6 3.6 collective-permute-start.5
  35.9 82.2 %all-reduce.9 = (f32[8]{0:T(128)S(1)}, f32[8]{0:T(128)S(1)}) all-reduce(f32[8]{0:T(128)S(1)} %get-tuple-element.19, f32[8]{0:T(128)S(1)} %get-tuple-element.18), channel_id=1, replica_groups=mesh['gx'=16,'gy'=16] {'gx','gy'}, use_global_device_ids=true, to_apply=%region_1.2 | all-reduce | flops 16 | bytes 128 | tf_op jit(solution)/shard_map/psum | solution.py:78
  121.8 4.7 %collective-permute-start.7 = (f32[8,1,16,256]{3,2,1,0:T(8,128)}, f32[8,1,16,256]{3,2,1,0:T(8,128)}, u32[]{:S(2)}, u32[]{:S(2)}) collective-permute-start(f32[8,1,16,256]{3,2,1,0:T(8,128)} %get-tuple-element.44), channel_id=1, source_target_pairs={{0,16},{16,32},{32,48},{48,64},{64,80},{80,96},{96,112},{112,128},... | collective-permute-start | bytes 393224 | tf_op jit(solution)/shard_map/ppermute | solution.py:25
  133.0 9.7 %reshape.75 = f32[4,2,8,2,128,2]{5,4,3,2,1,0:T(8,128)} reshape(f32[8,16,256]{2,1,0:T(8,128)S(1)} %broadcast_select_fusion.1) | data formatting | bytes 262144 | tf_op jit(solution)/shard_map/reshape | solution.py:91
  143.8 3.4 collective-permute-start.8
  147.2 2.9 collective-permute-start.9
  156.1 9.8 %reshape.76 = f32[4,2,8,2,128,2]{5,4,3,2,1,0:T(8,128)} reshape(f32[8,16,256]{2,1,0:T(8,128)S(1)} %broadcast_select_fusion) | data formatting | bytes 262144 | tf_op jit(solution)/shard_map/reshape | solution.py:92
  166.1 5.3 %fusion.13 = f32[8,8,16,256]{3,2,1,0:T(8,128)S(1)} fusion(f32[8,8,16,256]{3,2,1,0:T(8,128)} %copy-done.1, f32[8,8,16,256]{3,2,1,0:T(8,128)S(1)} %get-tuple-element.27, f32[8,10,1,256]{3,2,1,0:T(1,128)S(1)} %copy.441, f32[8,1,16,256]{3,2,1,0:T(8,128)} %copy-done.25, f32[8,1,16,256]{3,2,1,0:T(8,128)} %collective-permute-done.7, ...), kind=kLoop, calls=%fused_computation.28 | loop fusion | flops 6553600 | bytes 4489216 | tf_op jit(solution)/shard_map/add | solution.py:72
  173.4 4.7 %collective-permute-start.11 = (f32[8,1,16,256]{3,2,1,0:T(8,128)}, f32[8,1,16,256]{3,2,1,0:T(8,128)}, u32[]{:S(2)}, u32[]{:S(2)}) collective-permute-start(f32[8,1,16,256]{3,2,1,0:T(8,128)} %get-tuple-element.42), channel_id=1, source_target_pairs={{0,16},{16,32},{32,48},{48,64},{64,80},{80,96},{96,112},{112,128},... | collective-permute-start | bytes 393224 | tf_op jit(solution)/shard_map/ppermute | solution.py:25
  178.1 6.8 %slice_reduce_fusion = f32[4,8,128]{2,1,0:T(8,128)} fusion(f32[4,2,8,2,128,2]{5,4,3,2,1,0:T(8,128)} %reshape.76), kind=kLoop, calls=%fused_computation | loop fusion | flops 12288 | bytes 81920 | tf_op jit(solution)/shard_map/reduce_sum | solution.py:92
  184.8 10.5 %reshape.77 = f32[4,2,8,2,128,2]{5,4,3,2,1,0:T(8,128)} reshape(f32[8,16,256]{2,1,0:T(8,128)} %copy-done.8) | data formatting | bytes 262144 | tf_op jit(solution)/shard_map/reshape | solution.py:93
  195.3 4.6 %reduce_sum.69 = f32[4,8,128]{2,1,0:T(8,128)} reduce(f32[4,2,8,2,128,2]{5,4,3,2,1,0:T(8,128)} %reshape.77, f32[]{:T(128)} %constant.65.clone.1), dimensions={1,3,5}, to_apply=%region_8.9 | reduce | flops 28672 | bytes 147460 | tf_op jit(solution)/shard_map/reduce_sum | solution.py:93
  201.2 3.0 collective-permute-start.12
  211.3 9.8 %copy.446 = f32[8,8,16,256]{0,3,2,1:T(8,128)} copy(f32[8,8,16,256]{3,2,1,0:T(8,128)} %fusion.19) | data formatting | bytes 2097152 | tf_op jit(solution)/shard_map/sub | solution.py:128
  221.1 13.1 %reduce_sum.65 = f32[8,4,8,128]{0,3,2,1:T(8,128)} reduce(f32[8,4,2,8,2,128,2]{0,6,5,4,3,2,1:T(2,128)} %bitcast.30, f32[]{:T(128)} %constant.65.clone.1), dimensions={2,4,6}, to_apply=%region_4.5 | reduce | flops 229376 | bytes 1179652 | tf_op jit(solution)/shard_map/reduce_sum | solution.py:99
  239.4 4.0 collective-permute-start.17
  244.4 2.9 collective-permute-start.18
  247.4 4.3 %collective-permute-start.19 = (f32[8,6,1,128]{3,2,1,0:T(1,128)S(1)}, f32[8,6,1,128]{3,2,1,0:T(1,128)S(1)}, u32[]{:S(2)}, u32[]{:S(2)}) collective-permute-start(f32[8,6,1,128]{3,2,1,0:T(1,128)S(1)} %get-tuple-element.53), channel_id=1, source_target_pairs={{0,1},{1,2},{2,3},{3,4},{4,5},{5,6},{6,7},{7,8},{8,9},{9,10},{10,1... | collective-permute-start | bytes 73736 | tf_op jit(solution)/shard_map/ppermute | solution.py:25
  255.1 4.6 %collective-permute-start.21 = (f32[8,1,8,128]{3,2,1,0:T(8,128)S(1)}, f32[8,1,8,128]{3,2,1,0:T(8,128)S(1)}, u32[]{:S(2)}, u32[]{:S(2)}) collective-permute-start(f32[8,1,8,128]{3,2,1,0:T(8,128)S(1)} %get-tuple-element.56), channel_id=1, source_target_pairs={{0,16},{16,32},{32,48},{48,64},{64,80},{80,96},{96,112},{112,128},... | collective-permute-start | bytes 98312 | tf_op jit(solution)/shard_map/ppermute | solution.py:25
  262.6 5.1 %collective-permute-start.23 = (f32[8,6,1,128]{3,2,1,0:T(1,128)S(1)}, f32[8,6,1,128]{3,2,1,0:T(1,128)S(1)}, u32[]{:S(2)}, u32[]{:S(2)}) collective-permute-start(f32[8,6,1,128]{3,2,1,0:T(1,128)S(1)} %get-tuple-element.51), channel_id=1, source_target_pairs={{0,1},{1,2},{2,3},{3,4},{4,5},{5,6},{6,7},{7,8},{8,9},{9,10},{10,1... | collective-permute-start | bytes 73736 | tf_op jit(solution)/shard_map/ppermute | solution.py:25
  270.1 4.6 %collective-permute-start.25 = (f32[8,1,8,128]{3,2,1,0:T(8,128)S(1)}, f32[8,1,8,128]{3,2,1,0:T(8,128)S(1)}, u32[]{:S(2)}, u32[]{:S(2)}) collective-permute-start(f32[8,1,8,128]{3,2,1,0:T(8,128)S(1)} %get-tuple-element.54), channel_id=1, source_target_pairs={{0,16},{16,32},{32,48},{48,64},{64,80},{80,96},{96,112},{112,128},... | collective-permute-start | bytes 98312 | tf_op jit(solution)/shard_map/ppermute | solution.py:25
  277.7 5.1 %collective-permute-start.27 = (f32[8,6,1,128]{3,2,1,0:T(1,128)S(1)}, f32[8,6,1,128]{3,2,1,0:T(1,128)S(1)}, u32[]{:S(2)}, u32[]{:S(2)}) collective-permute-start(f32[8,6,1,128]{3,2,1,0:T(1,128)S(1)} %get-tuple-element.49), channel_id=1, source_target_pairs={{0,1},{1,2},{2,3},{3,4},{4,5},{5,6},{6,7},{7,8},{8,9},{9,10},{10,1... | collective-permute-start | bytes 73736 | tf_op jit(solution)/shard_map/ppermute | solution.py:25
  287.4 7.1 %broadcast_in_dim.30 = f32[8,4,2,8,2,128,2]{0,6,5,4,3,2,1:T(2,128)} broadcast(f32[8,4,8,128]{0,3,2,1:T(8,128)} %copy.451), dimensions={0,1,3,5} | broadcast | bytes 1179648 | tf_op jit(solution)/shard_map/broadcast_in_dim | solution.py:104
  294.5 10.6 %copy.452 = f32[8,8,16,256]{3,2,1,0:T(8,128)} copy(f32[8,8,16,256]{0,3,2,1:T(8,128)} %bitcast.31) | data formatting | bytes 2097152 | tf_op jit(solution)/shard_map/reshape | solution.py:104
  308.1 4.6 %collective-permute-start.29 = (f32[8,1,16,256]{3,2,1,0:T(8,128)S(1)}, f32[8,1,16,256]{3,2,1,0:T(8,128)S(1)}, u32[]{:S(2)}, u32[]{:S(2)}) collective-permute-start(f32[8,1,16,256]{3,2,1,0:T(8,128)S(1)} %get-tuple-element.40), channel_id=1, source_target_pairs={{0,16},{16,32},{32,48},{48,64},{64,80},{80,96},{96,112},{112,128},... | collective-permute-start | bytes 393224 | tf_op jit(solution)/shard_map/ppermute | solution.py:25
  316.7 5.3 %collective-permute-start.31 = (f32[8,10,1,256]{3,0,2,1:T(8,128)S(1)}, f32[8,10,1,256]{3,0,2,1:T(8,128)S(1)}, u32[]{:S(2)}, u32[]{:S(2)}) collective-permute-start(f32[8,10,1,256]{3,0,2,1:T(8,128)S(1)} %copy.455), channel_id=1, source_target_pairs={{0,1},{1,2},{2,3},{3,4},{4,5},{5,6},{6,7},{7,8},{8,9},{9,10},{10,1... | collective-permute-start | bytes 245768 | tf_op jit(solution)/shard_map/ppermute | solution.py:25
  324.9 3.0 convolution_bitcast_fusion
  327.9 93.9 %psum.23 = f32[8,8]{0,1:T(8,128)S(1)} all-reduce(f32[8,8]{0,1:T(8,128)S(1)} %convolution_bitcast_fusion), channel_id=1, replica_groups=mesh['gx'=16,'gy'=16] {'gx','gy'}, use_global_device_ids=true, to_apply=%region_9.10 | all-reduce | flops 64 | bytes 512 | tf_op jit(solution)/shard_map/psum | solution.py:142
  (190 shorter events, 75.3 us)
Async XLA Ops:
  1.7 30.6 %collective-permute-start = (f32[1,16,256]{2,1,0:T(8,128)S(1)}, f32[1,16,256]{2,1,0:T(8,128)S(1)}, u32[]{:S(2)}, u32[]{:S(2)}) collective-permute-start(f32[1,16,256]{2,1,0:T(8,128)S(1)} %slice.372), channel_id=1, source_target_pairs={{0,16},{16,32},{32,48},{48,64},{64,80},{80,96},{96,112},{112,128},... | collective-permute-start | bytes 49160 | tf_op jit(solution)/shard_map/ppermute | solution.py:14
  6.6 25.6 %collective-permute-start.1 = (f32[8,1,256]{2,1,0:T(1,128)S(1)}, f32[8,1,256]{2,1,0:T(1,128)S(1)}, u32[]{:S(2)}, u32[]{:S(2)}) collective-permute-start(f32[8,1,256]{2,1,0:T(1,128)S(1)} %slice.374), channel_id=1, source_target_pairs={{0,1},{1,2},{2,3},{3,4},{4,5},{5,6},{6,7},{7,8},{8,9},{9,10},{10,1... | collective-permute-start | bytes 24584 | tf_op jit(solution)/shard_map/ppermute | solution.py:14
  12.0 14.3 %collective-permute-start.3 = (f32[8,1,16,256]{3,2,1,0:T(8,128)S(1)}, f32[8,1,16,256]{3,2,1,0:T(8,128)S(1)}, u32[]{:S(2)}, u32[]{:S(2)}) collective-permute-start(f32[8,1,16,256]{3,2,1,0:T(8,128)S(1)} %get-tuple-element.47), channel_id=1, source_target_pairs={{0,16},{16,32},{32,48},{48,64},{64,80},{80,96},{96,112},{112,128},... | collective-permute-start | bytes 393224 | tf_op jit(solution)/shard_map/ppermute | solution.py:25
  15.2 11.3 %collective-permute-start.2 = (f32[8,1,16,256]{3,2,1,0:T(8,128)S(1)}, f32[8,1,16,256]{3,2,1,0:T(8,128)S(1)}, u32[]{:S(2)}, u32[]{:S(2)}) collective-permute-start(f32[8,1,16,256]{3,2,1,0:T(8,128)S(1)} %get-tuple-element.46), channel_id=1, source_target_pairs={{16,0},{32,16},{48,32},{64,48},{80,64},{96,80},{112,96},{128,112},... | collective-permute-start | bytes 393224 | tf_op jit(solution)/shard_map/ppermute | solution.py:27
  26.6 6.4 %collective-permute-start.4 = (f32[8,10,1,256]{3,0,2,1:T(8,128)S(1)}, f32[8,10,1,256]{3,0,2,1:T(8,128)S(1)}, u32[]{:S(2)}, u32[]{:S(2)}) collective-permute-start(f32[8,10,1,256]{3,0,2,1:T(8,128)S(1)} %copy.466), channel_id=1, source_target_pairs={{1,0},{2,1},{3,2},{4,3},{5,4},{6,5},{7,6},{8,7},{9,8},{10,9},{11,1... | collective-permute-start | bytes 245768 | tf_op jit(solution)/shard_map/ppermute | solution.py:27
  28.6 5.1 %collective-permute-start.5 = (f32[8,10,1,256]{3,0,2,1:T(8,128)S(1)}, f32[8,10,1,256]{3,0,2,1:T(8,128)S(1)}, u32[]{:S(2)}, u32[]{:S(2)}) collective-permute-start(f32[8,10,1,256]{3,0,2,1:T(8,128)S(1)} %copy.467), channel_id=1, source_target_pairs={{0,1},{1,2},{2,3},{3,4},{4,5},{5,6},{6,7},{7,8},{8,9},{9,10},{10,1... | collective-permute-start | bytes 245768 | tf_op jit(solution)/shard_map/ppermute | solution.py:25
  120.6 22.2 %collective-permute-start.6 = (f32[8,1,16,256]{3,2,1,0:T(8,128)}, f32[8,1,16,256]{3,2,1,0:T(8,128)S(1)}, u32[]{:S(2)}, u32[]{:S(2)}) collective-permute-start(f32[8,1,16,256]{3,2,1,0:T(8,128)} %get-tuple-element.45), channel_id=1, source_target_pairs={{16,0},{32,16},{48,32},{64,48},{80,64},{96,80},{112,96},{128,112},... | collective-permute-start | bytes 393224 | tf_op jit(solution)/shard_map/ppermute | solution.py:27
  121.8 20.9 %collective-permute-start.7 = (f32[8,1,16,256]{3,2,1,0:T(8,128)}, f32[8,1,16,256]{3,2,1,0:T(8,128)}, u32[]{:S(2)}, u32[]{:S(2)}) collective-permute-start(f32[8,1,16,256]{3,2,1,0:T(8,128)} %get-tuple-element.44), channel_id=1, source_target_pairs={{0,16},{16,32},{32,48},{48,64},{64,80},{80,96},{96,112},{112,128},... | collective-permute-start | bytes 393224 | tf_op jit(solution)/shard_map/ppermute | solution.py:25
  130.5 76.3 %collective-permute-start.14 = (f32[1,8,128]{2,1,0:T(8,128)}, f32[1,8,128]{2,1,0:T(8,128)}, u32[]{:S(2)}, u32[]{:S(2)}) collective-permute-start(f32[1,8,128]{2,1,0:T(8,128)} %slice.384), channel_id=1, source_target_pairs={{0,16},{16,32},{32,48},{48,64},{64,80},{80,96},{96,112},{112,128},... | collective-permute-start | bytes 12296 | tf_op jit(solution)/shard_map/ppermute | solution.py:14
  143.8 22.1 %collective-permute-start.8 = (f32[8,10,1,256]{3,0,2,1:T(8,128)S(1)}, f32[8,10,1,256]{3,0,2,1:T(8,128)S(1)}, u32[]{:S(2)}, u32[]{:S(2)}) collective-permute-start(f32[8,10,1,256]{3,0,2,1:T(8,128)S(1)} %copy.438), channel_id=1, source_target_pairs={{1,0},{2,1},{3,2},{4,3},{5,4},{6,5},{7,6},{8,7},{9,8},{10,9},{11,1... | collective-permute-start | bytes 245768 | tf_op jit(solution)/shard_map/ppermute | solution.py:27
  147.2 18.7 %collective-permute-start.9 = (f32[8,10,1,256]{3,0,2,1:T(8,128)S(1)}, f32[8,10,1,256]{3,0,2,1:T(8,128)S(1)}, u32[]{:S(2)}, u32[]{:S(2)}) collective-permute-start(f32[8,10,1,256]{3,0,2,1:T(8,128)S(1)} %copy.440), channel_id=1, source_target_pairs={{0,1},{1,2},{2,3},{3,4},{4,5},{5,6},{6,7},{7,8},{8,9},{9,10},{10,1... | collective-permute-start | bytes 245768 | tf_op jit(solution)/shard_map/ppermute | solution.py:25
  153.5 53.3 %collective-permute-start.15 = (f32[4,1,128]{2,1,0:T(1,128)}, f32[4,1,128]{2,1,0:T(1,128)}, u32[]{:S(2)}, u32[]{:S(2)}) collective-permute-start(f32[4,1,128]{2,1,0:T(1,128)} %slice.387), channel_id=1, source_target_pairs={{0,1},{1,2},{2,3},{3,4},{4,5},{5,6},{6,7},{7,8},{8,9},{9,10},{10,1... | collective-permute-start | bytes 6152 | tf_op jit(solution)/shard_map/ppermute | solution.py:14
  172.1 27.9 %collective-permute-start.10 = (f32[8,1,16,256]{3,2,1,0:T(8,128)}, f32[8,1,16,256]{3,2,1,0:T(8,128)}, u32[]{:S(2)}, u32[]{:S(2)}) collective-permute-start(f32[8,1,16,256]{3,2,1,0:T(8,128)} %get-tuple-element.43), channel_id=1, source_target_pairs={{16,0},{32,16},{48,32},{64,48},{80,64},{96,80},{112,96},{128,112},... | collective-permute-start | bytes 393224 | tf_op jit(solution)/shard_map/ppermute | solution.py:27
  173.4 26.6 %collective-permute-start.11 = (f32[8,1,16,256]{3,2,1,0:T(8,128)}, f32[8,1,16,256]{3,2,1,0:T(8,128)}, u32[]{:S(2)}, u32[]{:S(2)}) collective-permute-start(f32[8,1,16,256]{3,2,1,0:T(8,128)} %get-tuple-element.42), channel_id=1, source_target_pairs={{0,16},{16,32},{32,48},{48,64},{64,80},{80,96},{96,112},{112,128},... | collective-permute-start | bytes 393224 | tf_op jit(solution)/shard_map/ppermute | solution.py:25
  201.2 7.0 %collective-permute-start.12 = (f32[8,10,1,256]{3,0,2,1:T(8,128)S(1)}, f32[8,10,1,256]{3,0,2,1:T(8,128)S(1)}, u32[]{:S(2)}, u32[]{:S(2)}) collective-permute-start(f32[8,10,1,256]{3,0,2,1:T(8,128)S(1)} %copy.442), channel_id=1, source_target_pairs={{1,0},{2,1},{3,2},{4,3},{5,4},{6,5},{7,6},{8,7},{9,8},{10,9},{11,1... | collective-permute-start | bytes 245768 | tf_op jit(solution)/shard_map/ppermute | solution.py:27
  204.3 4.1 collective-permute-start.13
  238.1 5.3 %collective-permute-start.16 = (f32[8,1,8,128]{3,2,1,0:T(8,128)S(1)}, f32[8,1,8,128]{3,2,1,0:T(8,128)S(1)}, u32[]{:S(2)}, u32[]{:S(2)}) collective-permute-start(f32[8,1,8,128]{3,2,1,0:T(8,128)S(1)} %get-tuple-element.59), channel_id=1, source_target_pairs={{16,0},{32,16},{48,32},{64,48},{80,64},{96,80},{112,96},{128,112},... | collective-permute-start | bytes 98312 | tf_op jit(solution)/shard_map/ppermute | solution.py:27
  239.4 5.0 %collective-permute-start.17 = (f32[8,1,8,128]{3,2,1,0:T(8,128)S(1)}, f32[8,1,8,128]{3,2,1,0:T(8,128)S(1)}, u32[]{:S(2)}, u32[]{:S(2)}) collective-permute-start(f32[8,1,8,128]{3,2,1,0:T(8,128)S(1)} %get-tuple-element.58), channel_id=1, source_target_pairs={{0,16},{16,32},{32,48},{48,64},{64,80},{80,96},{96,112},{112,128},... | collective-permute-start | bytes 98312 | tf_op jit(solution)/shard_map/ppermute | solution.py:25
  244.4 7.3 %collective-permute-start.18 = (f32[8,6,1,128]{3,2,1,0:T(1,128)S(1)}, f32[8,6,1,128]{3,2,1,0:T(1,128)S(1)}, u32[]{:S(2)}, u32[]{:S(2)}) collective-permute-start(f32[8,6,1,128]{3,2,1,0:T(1,128)S(1)} %get-tuple-element.52), channel_id=1, source_target_pairs={{1,0},{2,1},{3,2},{4,3},{5,4},{6,5},{7,6},{8,7},{9,8},{10,9},{11,1... | collective-permute-start | bytes 73736 | tf_op jit(solution)/shard_map/ppermute | solution.py:27
  247.4 5.3 %collective-permute-start.19 = (f32[8,6,1,128]{3,2,1,0:T(1,128)S(1)}, f32[8,6,1,128]{3,2,1,0:T(1,128)S(1)}, u32[]{:S(2)}, u32[]{:S(2)}) collective-permute-start(f32[8,6,1,128]{3,2,1,0:T(1,128)S(1)} %get-tuple-element.53), channel_id=1, source_target_pairs={{0,1},{1,2},{2,3},{3,4},{4,5},{5,6},{6,7},{7,8},{8,9},{9,10},{10,1... | collective-permute-start | bytes 73736 | tf_op jit(solution)/shard_map/ppermute | solution.py:25
  253.8 5.9 %collective-permute-start.20 = (f32[8,1,8,128]{3,2,1,0:T(8,128)S(1)}, f32[8,1,8,128]{3,2,1,0:T(8,128)S(1)}, u32[]{:S(2)}, u32[]{:S(2)}) collective-permute-start(f32[8,1,8,128]{3,2,1,0:T(8,128)S(1)} %get-tuple-element.57), channel_id=1, source_target_pairs={{16,0},{32,16},{48,32},{64,48},{80,64},{96,80},{112,96},{128,112},... | collective-permute-start | bytes 98312 | tf_op jit(solution)/shard_map/ppermute | solution.py:27
  255.1 5.6 %collective-permute-start.21 = (f32[8,1,8,128]{3,2,1,0:T(8,128)S(1)}, f32[8,1,8,128]{3,2,1,0:T(8,128)S(1)}, u32[]{:S(2)}, u32[]{:S(2)}) collective-permute-start(f32[8,1,8,128]{3,2,1,0:T(8,128)S(1)} %get-tuple-element.56), channel_id=1, source_target_pairs={{0,16},{16,32},{32,48},{48,64},{64,80},{80,96},{96,112},{112,128},... | collective-permute-start | bytes 98312 | tf_op jit(solution)/shard_map/ppermute | solution.py:25
  260.7 7.0 %collective-permute-start.22 = (f32[8,6,1,128]{3,2,1,0:T(1,128)S(1)}, f32[8,6,1,128]{3,2,1,0:T(1,128)S(1)}, u32[]{:S(2)}, u32[]{:S(2)}) collective-permute-start(f32[8,6,1,128]{3,2,1,0:T(1,128)S(1)} %get-tuple-element.50), channel_id=1, source_target_pairs={{1,0},{2,1},{3,2},{4,3},{5,4},{6,5},{7,6},{8,7},{9,8},{10,9},{11,1... | collective-permute-start | bytes 73736 | tf_op jit(solution)/shard_map/ppermute | solution.py:27
  262.6 6.0 %collective-permute-start.23 = (f32[8,6,1,128]{3,2,1,0:T(1,128)S(1)}, f32[8,6,1,128]{3,2,1,0:T(1,128)S(1)}, u32[]{:S(2)}, u32[]{:S(2)}) collective-permute-start(f32[8,6,1,128]{3,2,1,0:T(1,128)S(1)} %get-tuple-element.51), channel_id=1, source_target_pairs={{0,1},{1,2},{2,3},{3,4},{4,5},{5,6},{6,7},{7,8},{8,9},{9,10},{10,1... | collective-permute-start | bytes 73736 | tf_op jit(solution)/shard_map/ppermute | solution.py:25
  268.8 5.9 %collective-permute-start.24 = (f32[8,1,8,128]{3,2,1,0:T(8,128)S(1)}, f32[8,1,8,128]{3,2,1,0:T(8,128)S(1)}, u32[]{:S(2)}, u32[]{:S(2)}) collective-permute-start(f32[8,1,8,128]{3,2,1,0:T(8,128)S(1)} %get-tuple-element.55), channel_id=1, source_target_pairs={{16,0},{32,16},{48,32},{64,48},{80,64},{96,80},{112,96},{128,112},... | collective-permute-start | bytes 98312 | tf_op jit(solution)/shard_map/ppermute | solution.py:27
  270.1 5.6 %collective-permute-start.25 = (f32[8,1,8,128]{3,2,1,0:T(8,128)S(1)}, f32[8,1,8,128]{3,2,1,0:T(8,128)S(1)}, u32[]{:S(2)}, u32[]{:S(2)}) collective-permute-start(f32[8,1,8,128]{3,2,1,0:T(8,128)S(1)} %get-tuple-element.54), channel_id=1, source_target_pairs={{0,16},{16,32},{32,48},{48,64},{64,80},{80,96},{96,112},{112,128},... | collective-permute-start | bytes 98312 | tf_op jit(solution)/shard_map/ppermute | solution.py:25
  275.8 7.0 %collective-permute-start.26 = (f32[8,6,1,128]{3,2,1,0:T(1,128)S(1)}, f32[8,6,1,128]{3,2,1,0:T(1,128)S(1)}, u32[]{:S(2)}, u32[]{:S(2)}) collective-permute-start(f32[8,6,1,128]{3,2,1,0:T(1,128)S(1)} %get-tuple-element.48), channel_id=1, source_target_pairs={{1,0},{2,1},{3,2},{4,3},{5,4},{6,5},{7,6},{8,7},{9,8},{10,9},{11,1... | collective-permute-start | bytes 73736 | tf_op jit(solution)/shard_map/ppermute | solution.py:27
  277.7 6.0 %collective-permute-start.27 = (f32[8,6,1,128]{3,2,1,0:T(1,128)S(1)}, f32[8,6,1,128]{3,2,1,0:T(1,128)S(1)}, u32[]{:S(2)}, u32[]{:S(2)}) collective-permute-start(f32[8,6,1,128]{3,2,1,0:T(1,128)S(1)} %get-tuple-element.49), channel_id=1, source_target_pairs={{0,1},{1,2},{2,3},{3,4},{4,5},{5,6},{6,7},{7,8},{8,9},{9,10},{10,1... | collective-permute-start | bytes 73736 | tf_op jit(solution)/shard_map/ppermute | solution.py:25
  306.6 6.5 %collective-permute-start.28 = (f32[8,1,16,256]{3,2,1,0:T(8,128)S(1)}, f32[8,1,16,256]{3,2,1,0:T(8,128)S(1)}, u32[]{:S(2)}, u32[]{:S(2)}) collective-permute-start(f32[8,1,16,256]{3,2,1,0:T(8,128)S(1)} %get-tuple-element.41), channel_id=1, source_target_pairs={{16,0},{32,16},{48,32},{64,48},{80,64},{96,80},{112,96},{128,112},... | collective-permute-start | bytes 393224 | tf_op jit(solution)/shard_map/ppermute | solution.py:27
  308.1 6.5 %collective-permute-start.29 = (f32[8,1,16,256]{3,2,1,0:T(8,128)S(1)}, f32[8,1,16,256]{3,2,1,0:T(8,128)S(1)}, u32[]{:S(2)}, u32[]{:S(2)}) collective-permute-start(f32[8,1,16,256]{3,2,1,0:T(8,128)S(1)} %get-tuple-element.40), channel_id=1, source_target_pairs={{0,16},{16,32},{32,48},{48,64},{64,80},{80,96},{96,112},{112,128},... | collective-permute-start | bytes 393224 | tf_op jit(solution)/shard_map/ppermute | solution.py:25
  314.7 7.2 %collective-permute-start.30 = (f32[8,10,1,256]{3,0,2,1:T(8,128)S(1)}, f32[8,10,1,256]{3,0,2,1:T(8,128)S(1)}, u32[]{:S(2)}, u32[]{:S(2)}) collective-permute-start(f32[8,10,1,256]{3,0,2,1:T(8,128)S(1)} %copy.453), channel_id=1, source_target_pairs={{1,0},{2,1},{3,2},{4,3},{5,4},{6,5},{7,6},{8,7},{9,8},{10,9},{11,1... | collective-permute-start | bytes 245768 | tf_op jit(solution)/shard_map/ppermute | solution.py:27
  316.7 6.5 %collective-permute-start.31 = (f32[8,10,1,256]{3,0,2,1:T(8,128)S(1)}, f32[8,10,1,256]{3,0,2,1:T(8,128)S(1)}, u32[]{:S(2)}, u32[]{:S(2)}) collective-permute-start(f32[8,10,1,256]{3,0,2,1:T(8,128)S(1)} %copy.455), channel_id=1, source_target_pairs={{0,1},{1,2},{2,3},{3,4},{4,5},{5,6},{6,7},{7,8},{8,9},{9,10},{10,1... | collective-permute-start | bytes 245768 | tf_op jit(solution)/shard_map/ppermute | solution.py:25
  (37 other events, 579.5 us)
where the time goes:
time: 429 us; the launch traced here: 427 us
  blocking collectives  176 us (41%)
  starting transfers between devices  98.6 us (23%)
  local copies, waits for them, and re-layouts  80.4 us (19%)
  other arithmetic  57.3 us (13%)
  waiting for transfers between devices  9.35 us (2%)
    psum x1, blocking collectives, per_device(): gram = lax.psum(local_gram, ('gx', 'gy'))  93.9 us
    psum x1, blocking collectives, rayleigh_sums(): lax.psum((jnp.sum(vectors * applied, axis=(1, 2, 3)), jnp.sum(vectors * (...  82.2 us
    ppermute x14, starting transfers between devices, with_halo(): lax.ppermute(tail, axis, [(i, (i + 1) % count) for i in range(ends)])  59 us
    ppermute x14, starting transfers between devices, with_halo(): lax.ppermute(head, axis, [((i + 1) % count, i) for i in range(ends)])  26.2 us
    ppermute x4, starting transfers between devices, shifted(): return lax.ppermute(shard, axis, pairs)  13.3 us
    reduce_sum x1, other arithmetic, restrict(): field.reshape(kk, sx // 2, 2, sy // 2, 2, sz // 2, 2).sum(axis=(2, 4, 6))  13.1 us
    reshape x1, local copies, waits for them, and re-layouts, prolong(): jnp.broadcast_to(field[:, :, None, :, None, :, None], (kk, sx, 2, sy, 2,...  10.6 us
    reshape x1, local copies, waits for them, and re-layouts, coarse_weights(): dsum = degree.reshape(shape).sum(axis=(1, 3, 5))  10.5 us
  transfers between devices with their start and end apart: 32, of which 10 were waited for; matrix products, arithmetic and copies ran while one was open for 17% of the time, Pallas kernels for 0%

commit v1 on v0

--- a/solution.py
+++ b/solution.py
@@ -6,6 +6,11 @@
 COARSE_SWEEPS = 4
 OMEGA = 0.8
 SHIFT = 0.1
+
+
+def summed_here(x, axis):
+    parts = lax.all_gather(x, axis)
+    return jnp.sum(parts, axis=0)
 
 
 def shifted(shard, axis, by):
@@ -139,7 +144,7 @@
     local_gram = jnp.einsum(
         "aijk,bijk->ab", updated, degree[None] * updated, precision=lax.Precision.HIGHEST
     )
-    gram = lax.psum(local_gram, ("gx", "gy"))
+    gram = summed_here(local_gram, ("gx", "gy"))
     gram = gram / (span_x * span_y * depth)
     chol = jnp.linalg.cholesky(gram)
     flat = updated.reshape(updated.shape[0], -1)

time: 429 us -> 415 us (0.967)
  blocking collectives: 176 us -> 162 us
    psum x1 -> x0, blocking collectives: 93.9 us -> none  [per_device(): gram = lax.psum(local_gram, ('gx', 'gy'))]
    all_gather x0 -> x1, blocking collectives: none -> 79.8 us  [summed_here(): parts = lax.all_gather(x, axis)]
where the time goes in v1:
time: 415 us; the launch traced here: 413 us
  blocking collectives  162 us (39%)
  starting transfers between devices  98.6 us (24%)
  local copies, waits for them, and re-layouts  80.4 us (19%)
  other arithmetic  57.3 us (14%)
  waiting for transfers between devices  9.35 us (2%)
    psum x1, blocking collectives, rayleigh_sums(): lax.psum((jnp.sum(vectors * applied, axis=(1, 2, 3)), jnp.sum(vectors * (...  82.2 us
    all_gather x1, blocking collectives, summed_here(): parts = lax.all_gather(x, axis)  79.8 us
    ppermute x14, starting transfers between devices, with_halo(): lax.ppermute(tail, axis, [(i, (i + 1) % count) for i in range(ends)])  59 us
    ppermute x14, starting transfers between devices, with_halo(): lax.ppermute(head, axis, [((i + 1) % count, i) for i in range(ends)])  26.2 us
    ppermute x4, starting transfers between devices, shifted(): return lax.ppermute(shard, axis, pairs)  13.3 us
    reduce_sum x1, other arithmetic, restrict(): field.reshape(kk, sx // 2, 2, sy // 2, 2, sz // 2, 2).sum(axis=(2, 4, 6))  13.1 us
    reshape x1, local copies, waits for them, and re-layouts, prolong(): jnp.broadcast_to(field[:, :, None, :, None, :, None], (kk, sx, 2, sy, 2,...  10.6 us
    reshape x1, local copies, waits for them, and re-layouts, coarse_weights(): dsum = degree.reshape(shape).sum(axis=(1, 3, 5))  10.5 us
  transfers between devices with their start and end apart: 32, of which 10 were waited for; matrix products, arithmetic and copies ran while one was open for 17% of the time, Pallas kernels for 0%

profile of v1, /device:TPU:1, one launch (start us, length us, event | category | flops | bytes accessed | tf_op | source)
XLA Modules:
  0.0 413.4 jit_solution(17687440952845115915)
XLA Ops:
  1.7 3.9 collective-permute-start
  6.6 4.4 %collective-permute-start.1 = (f32[8,1,256]{2,1,0:T(1,128)S(1)}, f32[8,1,256]{2,1,0:T(1,128)S(1)}, u32[]{:S(2)}, u32[]{:S(2)}) collective-permute-start(f32[8,1,256]{2,1,0:T(1,128)S(1)} %slice.374), channel_id=1, source_target_pairs={{0,1},{1,2},{2,3},{3,4},{4,5},{5,6},{6,7},{7,8},{8,9},{9,10},{10,1... | collective-permute-start | bytes 24584 | tf_op jit(solution)/shard_map/ppermute | solution.py:19
  12.0 3.1 collective-permute-start.3
  16.5 9.8 %reshape.74 = f32[4,2,8,2,128,2]{5,4,3,2,1,0:T(8,128)} reshape(f32[8,16,256]{2,1,0:T(8,128)S(1)} %broadcast_select_fusion.2) | data formatting | bytes 262144 | tf_op jit(solution)/shard_map/reshape | solution.py:95
  28.6 3.6 collective-permute-start.5
  35.9 82.2 %all-reduce.9 = (f32[8]{0:T(128)S(1)}, f32[8]{0:T(128)S(1)}) all-reduce(f32[8]{0:T(128)S(1)} %get-tuple-element.19, f32[8]{0:T(128)S(1)} %get-tuple-element.18), channel_id=1, replica_groups=mesh['gx'=16,'gy'=16] {'gx','gy'}, use_global_device_ids=true, to_apply=%region_1.2 | all-reduce | flops 16 | bytes 128 | tf_op jit(solution)/shard_map/psum | solution.py:83
  121.9 4.7 %collective-permute-start.7 = (f32[8,1,16,256]{3,2,1,0:T(8,128)}, f32[8,1,16,256]{3,2,1,0:T(8,128)}, u32[]{:S(2)}, u32[]{:S(2)}) collective-permute-start(f32[8,1,16,256]{3,2,1,0:T(8,128)} %get-tuple-element.44), channel_id=1, source_target_pairs={{0,16},{16,32},{32,48},{48,64},{64,80},{80,96},{96,112},{112,128},... | collective-permute-start | bytes 393224 | tf_op jit(solution)/shard_map/ppermute | solution.py:30
  133.0 9.7 %reshape.75 = f32[4,2,8,2,128,2]{5,4,3,2,1,0:T(8,128)} reshape(f32[8,16,256]{2,1,0:T(8,128)S(1)} %broadcast_select_fusion.1) | data formatting | bytes 262144 | tf_op jit(solution)/shard_map/reshape | solution.py:96
  143.8 3.4 collective-permute-start.8
  147.3 2.9 collective-permute-start.9
  156.1 9.8 %reshape.76 = f32[4,2,8,2,128,2]{5,4,3,2,1,0:T(8,128)} reshape(f32[8,16,256]{2,1,0:T(8,128)S(1)} %broadcast_select_fusion) | data formatting | bytes 262144 | tf_op jit(solution)/shard_map/reshape | solution.py:97
  166.1 5.0 %fusion.13 = f32[8,8,16,256]{3,2,1,0:T(8,128)S(1)} fusion(f32[8,8,16,256]{3,2,1,0:T(8,128)} %copy-done.1, f32[8,8,16,256]{3,2,1,0:T(8,128)S(1)} %get-tuple-element.27, f32[8,10,1,256]{3,2,1,0:T(1,128)S(1)} %copy.434, f32[8,1,16,256]{3,2,1,0:T(8,128)} %copy-done.25, f32[8,1,16,256]{3,2,1,0:T(8,128)} %collective-permute-done.7, ...), kind=kLoop, calls=%fused_computation.28 | loop fusion | flops 6553600 | bytes 4489216 | tf_op jit(solution)/shard_map/add | solution.py:77
  173.1 4.7 %collective-permute-start.11 = (f32[8,1,16,256]{3,2,1,0:T(8,128)}, f32[8,1,16,256]{3,2,1,0:T(8,128)}, u32[]{:S(2)}, u32[]{:S(2)}) collective-permute-start(f32[8,1,16,256]{3,2,1,0:T(8,128)} %get-tuple-element.42), channel_id=1, source_target_pairs={{0,16},{16,32},{32,48},{48,64},{64,80},{80,96},{96,112},{112,128},... | collective-permute-start | bytes 393224 | tf_op jit(solution)/shard_map/ppermute | solution.py:30
  177.7 6.8 %slice_reduce_fusion = f32[4,8,128]{2,1,0:T(8,128)} fusion(f32[4,2,8,2,128,2]{5,4,3,2,1,0:T(8,128)} %reshape.76), kind=kLoop, calls=%fused_computation | loop fusion | flops 12288 | bytes 81920 | tf_op jit(solution)/shard_map/reduce_sum | solution.py:97
  184.5 10.5 %reshape.77 = f32[4,2,8,2,128,2]{5,4,3,2,1,0:T(8,128)} reshape(f32[8,16,256]{2,1,0:T(8,128)} %copy-done.8) | data formatting | bytes 262144 | tf_op jit(solution)/shard_map/reshape | solution.py:98
  195.0 4.6 %reduce_sum.80 = f32[4,8,128]{2,1,0:T(8,128)} reduce(f32[4,2,8,2,128,2]{5,4,3,2,1,0:T(8,128)} %reshape.77, f32[]{:T(128)} %constant.66.clone.1), dimensions={1,3,5}, to_apply=%region_8.9 | reduce | flops 28672 | bytes 147460 | tf_op jit(solution)/shard_map/reduce_sum | solution.py:98
  200.9 3.0 collective-permute-start.12
  211.0 9.8 %copy.439 = f32[8,8,16,256]{0,3,2,1:T(8,128)} copy(f32[8,8,16,256]{3,2,1,0:T(8,128)} %fusion.19) | data formatting | bytes 2097152 | tf_op jit(solution)/shard_map/sub | solution.py:133
  220.8 13.1 %reduce_sum.76 = f32[8,4,8,128]{0,3,2,1:T(8,128)} reduce(f32[8,4,2,8,2,128,2]{0,6,5,4,3,2,1:T(2,128)} %bitcast.34, f32[]{:T(128)} %constant.66.clone.1), dimensions={2,4,6}, to_apply=%region_4.5 | reduce | flops 229376 | bytes 1179652 | tf_op jit(solution)/shard_map/reduce_sum | solution.py:104
  239.1 4.0 collective-permute-start.17
  244.1 2.9 collective-permute-start.18
  247.0 4.3 %collective-permute-start.19 = (f32[8,6,1,128]{3,2,1,0:T(1,128)S(1)}, f32[8,6,1,128]{3,2,1,0:T(1,128)S(1)}, u32[]{:S(2)}, u32[]{:S(2)}) collective-permute-start(f32[8,6,1,128]{3,2,1,0:T(1,128)S(1)} %get-tuple-element.53), channel_id=1, source_target_pairs={{0,1},{1,2},{2,3},{3,4},{4,5},{5,6},{6,7},{7,8},{8,9},{9,10},{10,1... | collective-permute-start | bytes 73736 | tf_op jit(solution)/shard_map/ppermute | solution.py:30
  254.7 4.6 %collective-permute-start.21 = (f32[8,1,8,128]{3,2,1,0:T(8,128)S(1)}, f32[8,1,8,128]{3,2,1,0:T(8,128)S(1)}, u32[]{:S(2)}, u32[]{:S(2)}) collective-permute-start(f32[8,1,8,128]{3,2,1,0:T(8,128)S(1)} %get-tuple-element.56), channel_id=1, source_target_pairs={{0,16},{16,32},{32,48},{48,64},{64,80},{80,96},{96,112},{112,128},... | collective-permute-start | bytes 98312 | tf_op jit(solution)/shard_map/ppermute | solution.py:30
  262.3 5.1 %collective-permute-start.23 = (f32[8,6,1,128]{3,2,1,0:T(1,128)S(1)}, f32[8,6,1,128]{3,2,1,0:T(1,128)S(1)}, u32[]{:S(2)}, u32[]{:S(2)}) collective-permute-start(f32[8,6,1,128]{3,2,1,0:T(1,128)S(1)} %get-tuple-element.51), channel_id=1, source_target_pairs={{0,1},{1,2},{2,3},{3,4},{4,5},{5,6},{6,7},{7,8},{8,9},{9,10},{10,1... | collective-permute-start | bytes 73736 | tf_op jit(solution)/shard_map/ppermute | solution.py:30
  269.8 4.6 %collective-permute-start.25 = (f32[8,1,8,128]{3,2,1,0:T(8,128)S(1)}, f32[8,1,8,128]{3,2,1,0:T(8,128)S(1)}, u32[]{:S(2)}, u32[]{:S(2)}) collective-permute-start(f32[8,1,8,128]{3,2,1,0:T(8,128)S(1)} %get-tuple-element.54), channel_id=1, source_target_pairs={{0,16},{16,32},{32,48},{48,64},{64,80},{80,96},{96,112},{112,128},... | collective-permute-start | bytes 98312 | tf_op jit(solution)/shard_map/ppermute | solution.py:30
  277.4 5.1 %collective-permute-start.27 = (f32[8,6,1,128]{3,2,1,0:T(1,128)S(1)}, f32[8,6,1,128]{3,2,1,0:T(1,128)S(1)}, u32[]{:S(2)}, u32[]{:S(2)}) collective-permute-start(f32[8,6,1,128]{3,2,1,0:T(1,128)S(1)} %get-tuple-element.49), channel_id=1, source_target_pairs={{0,1},{1,2},{2,3},{3,4},{4,5},{5,6},{6,7},{7,8},{8,9},{9,10},{10,1... | collective-permute-start | bytes 73736 | tf_op jit(solution)/shard_map/ppermute | solution.py:30
  287.0 7.1 %broadcast_in_dim.30 = f32[8,4,2,8,2,128,2]{0,6,5,4,3,2,1:T(2,128)} broadcast(f32[8,4,8,128]{0,3,2,1:T(8,128)} %copy.444), dimensions={0,1,3,5} | broadcast | bytes 1179648 | tf_op jit(solution)/shard_map/broadcast_in_dim | solution.py:109
  294.2 10.6 %copy.445 = f32[8,8,16,256]{3,2,1,0:T(8,128)} copy(f32[8,8,16,256]{0,3,2,1:T(8,128)} %bitcast.35) | data formatting | bytes 2097152 | tf_op jit(solution)/shard_map/reshape | solution.py:109
  307.7 4.6 %collective-permute-start.29 = (f32[8,1,16,256]{3,2,1,0:T(8,128)S(1)}, f32[8,1,16,256]{3,2,1,0:T(8,128)S(1)}, u32[]{:S(2)}, u32[]{:S(2)}) collective-permute-start(f32[8,1,16,256]{3,2,1,0:T(8,128)S(1)} %get-tuple-element.40), channel_id=1, source_target_pairs={{0,16},{16,32},{32,48},{48,64},{64,80},{80,96},{96,112},{112,128},... | collective-permute-start | bytes 393224 | tf_op jit(solution)/shard_map/ppermute | solution.py:30
  316.3 5.3 %collective-permute-start.31 = (f32[8,10,1,256]{3,0,2,1:T(8,128)S(1)}, f32[8,10,1,256]{3,0,2,1:T(8,128)S(1)}, u32[]{:S(2)}, u32[]{:S(2)}) collective-permute-start(f32[8,10,1,256]{3,0,2,1:T(8,128)S(1)} %copy.448), channel_id=1, source_target_pairs={{0,1},{1,2},{2,3},{3,4},{4,5},{5,6},{6,7},{7,8},{8,9},{9,10},{10,1... | collective-permute-start | bytes 245768 | tf_op jit(solution)/shard_map/ppermute | solution.py:30
  324.6 3.0 convolution_bitcast_fusion
  327.6 79.8 %all-gather = f32[2048,8]{1,0:T(8,128)S(1)} all-gather(f32[8,8]{1,0:T(8,128)S(1)} %convolution_bitcast_fusion), channel_id=2, replica_groups=mesh['gx'=16,'gy'=16] {'gx','gy'}, dimensions={0}, use_global_device_ids=true | all-gather | bytes 65792 | tf_op jit(solution)/shard_map/all_gather | solution.py:12
  (190 shorter events, 75.6 us)
Async XLA Ops:
  1.7 30.6 %collective-permute-start = (f32[1,16,256]{2,1,0:T(8,128)S(1)}, f32[1,16,256]{2,1,0:T(8,128)S(1)}, u32[]{:S(2)}, u32[]{:S(2)}) collective-permute-start(f32[1,16,256]{2,1,0:T(8,128)S(1)} %slice.372), channel_id=1, source_target_pairs={{0,16},{16,32},{32,48},{48,64},{64,80},{80,96},{96,112},{112,128},... | collective-permute-start | bytes 49160 | tf_op jit(solution)/shard_map/ppermute | solution.py:19
  6.6 25.6 %collective-permute-start.1 = (f32[8,1,256]{2,1,0:T(1,128)S(1)}, f32[8,1,256]{2,1,0:T(1,128)S(1)}, u32[]{:S(2)}, u32[]{:S(2)}) collective-permute-start(f32[8,1,256]{2,1,0:T(1,128)S(1)} %slice.374), channel_id=1, source_target_pairs={{0,1},{1,2},{2,3},{3,4},{4,5},{5,6},{6,7},{7,8},{8,9},{9,10},{10,1... | collective-permute-start | bytes 24584 | tf_op jit(solution)/shard_map/ppermute | solution.py:19
  12.0 14.3 %collective-permute-start.3 = (f32[8,1,16,256]{3,2,1,0:T(8,128)S(1)}, f32[8,1,16,256]{3,2,1,0:T(8,128)S(1)}, u32[]{:S(2)}, u32[]{:S(2)}) collective-permute-start(f32[8,1,16,256]{3,2,1,0:T(8,128)S(1)} %get-tuple-element.47), channel_id=1, source_target_pairs={{0,16},{16,32},{32,48},{48,64},{64,80},{80,96},{96,112},{112,128},... | collective-permute-start | bytes 393224 | tf_op jit(solution)/shard_map/ppermute | solution.py:30
  15.2 11.3 %collective-permute-start.2 = (f32[8,1,16,256]{3,2,1,0:T(8,128)S(1)}, f32[8,1,16,256]{3,2,1,0:T(8,128)S(1)}, u32[]{:S(2)}, u32[]{:S(2)}) collective-permute-start(f32[8,1,16,256]{3,2,1,0:T(8,128)S(1)} %get-tuple-element.46), channel_id=1, source_target_pairs={{16,0},{32,16},{48,32},{64,48},{80,64},{96,80},{112,96},{128,112},... | collective-permute-start | bytes 393224 | tf_op jit(solution)/shard_map/ppermute | solution.py:32
  26.6 6.4 %collective-permute-start.4 = (f32[8,10,1,256]{3,0,2,1:T(8,128)S(1)}, f32[8,10,1,256]{3,0,2,1:T(8,128)S(1)}, u32[]{:S(2)}, u32[]{:S(2)}) collective-permute-start(f32[8,10,1,256]{3,0,2,1:T(8,128)S(1)} %copy.457), channel_id=1, source_target_pairs={{1,0},{2,1},{3,2},{4,3},{5,4},{6,5},{7,6},{8,7},{9,8},{10,9},{11,1... | collective-permute-start | bytes 245768 | tf_op jit(solution)/shard_map/ppermute | solution.py:32
  28.6 5.1 %collective-permute-start.5 = (f32[8,10,1,256]{3,0,2,1:T(8,128)S(1)}, f32[8,10,1,256]{3,0,2,1:T(8,128)S(1)}, u32[]{:S(2)}, u32[]{:S(2)}) collective-permute-start(f32[8,10,1,256]{3,0,2,1:T(8,128)S(1)} %copy.458), channel_id=1, source_target_pairs={{0,1},{1,2},{2,3},{3,4},{4,5},{5,6},{6,7},{7,8},{8,9},{9,10},{10,1... | collective-permute-start | bytes 245768 | tf_op jit(solution)/shard_map/ppermute | solution.py:30
  120.6 22.2 %collective-permute-start.6 = (f32[8,1,16,256]{3,2,1,0:T(8,128)}, f32[8,1,16,256]{3,2,1,0:T(8,128)S(1)}, u32[]{:S(2)}, u32[]{:S(2)}) collective-permute-start(f32[8,1,16,256]{3,2,1,0:T(8,128)} %get-tuple-element.45), channel_id=1, source_target_pairs={{16,0},{32,16},{48,32},{64,48},{80,64},{96,80},{112,96},{128,112},... | collective-permute-start | bytes 393224 | tf_op jit(solution)/shard_map/ppermute | solution.py:32
  121.9 20.9 %collective-permute-start.7 = (f32[8,1,16,256]{3,2,1,0:T(8,128)}, f32[8,1,16,256]{3,2,1,0:T(8,128)}, u32[]{:S(2)}, u32[]{:S(2)}) collective-permute-start(f32[8,1,16,256]{3,2,1,0:T(8,128)} %get-tuple-element.44), channel_id=1, source_target_pairs={{0,16},{16,32},{32,48},{48,64},{64,80},{80,96},{96,112},{112,128},... | collective-permute-start | bytes 393224 | tf_op jit(solution)/shard_map/ppermute | solution.py:30
  130.5 76.0 %collective-permute-start.14 = (f32[1,8,128]{2,1,0:T(8,128)}, f32[1,8,128]{2,1,0:T(8,128)}, u32[]{:S(2)}, u32[]{:S(2)}) collective-permute-start(f32[1,8,128]{2,1,0:T(8,128)} %slice.384), channel_id=1, source_target_pairs={{0,16},{16,32},{32,48},{48,64},{64,80},{80,96},{96,112},{112,128},... | collective-permute-start | bytes 12296 | tf_op jit(solution)/shard_map/ppermute | solution.py:19
  143.8 22.1 %collective-permute-start.8 = (f32[8,10,1,256]{3,0,2,1:T(8,128)S(1)}, f32[8,10,1,256]{3,0,2,1:T(8,128)S(1)}, u32[]{:S(2)}, u32[]{:S(2)}) collective-permute-start(f32[8,10,1,256]{3,0,2,1:T(8,128)S(1)} %copy.431), channel_id=1, source_target_pairs={{1,0},{2,1},{3,2},{4,3},{5,4},{6,5},{7,6},{8,7},{9,8},{10,9},{11,1... | collective-permute-start | bytes 245768 | tf_op jit(solution)/shard_map/ppermute | solution.py:32
  147.3 18.7 %collective-permute-start.9 = (f32[8,10,1,256]{3,0,2,1:T(8,128)S(1)}, f32[8,10,1,256]{3,0,2,1:T(8,128)S(1)}, u32[]{:S(2)}, u32[]{:S(2)}) collective-permute-start(f32[8,10,1,256]{3,0,2,1:T(8,128)S(1)} %copy.433), channel_id=1, source_target_pairs={{0,1},{1,2},{2,3},{3,4},{4,5},{5,6},{6,7},{7,8},{8,9},{9,10},{10,1... | collective-permute-start | bytes 245768 | tf_op jit(solution)/shard_map/ppermute | solution.py:30
  153.6 52.9 %collective-permute-start.15 = (f32[4,1,128]{2,1,0:T(1,128)}, f32[4,1,128]{2,1,0:T(1,128)}, u32[]{:S(2)}, u32[]{:S(2)}) collective-permute-start(f32[4,1,128]{2,1,0:T(1,128)} %slice.387), channel_id=1, source_target_pairs={{0,1},{1,2},{2,3},{3,4},{4,5},{5,6},{6,7},{7,8},{8,9},{9,10},{10,1... | collective-permute-start | bytes 6152 | tf_op jit(solution)/shard_map/ppermute | solution.py:19
  171.8 27.9 %collective-permute-start.10 = (f32[8,1,16,256]{3,2,1,0:T(8,128)}, f32[8,1,16,256]{3,2,1,0:T(8,128)}, u32[]{:S(2)}, u32[]{:S(2)}) collective-permute-start(f32[8,1,16,256]{3,2,1,0:T(8,128)} %get-tuple-element.43), channel_id=1, source_target_pairs={{16,0},{32,16},{48,32},{64,48},{80,64},{96,80},{112,96},{128,112},... | collective-permute-start | bytes 393224 | tf_op jit(solution)/shard_map/ppermute | solution.py:32
  173.1 26.6 %collective-permute-start.11 = (f32[8,1,16,256]{3,2,1,0:T(8,128)}, f32[8,1,16,256]{3,2,1,0:T(8,128)}, u32[]{:S(2)}, u32[]{:S(2)}) collective-permute-start(f32[8,1,16,256]{3,2,1,0:T(8,128)} %get-tuple-element.42), channel_id=1, source_target_pairs={{0,16},{16,32},{32,48},{48,64},{64,80},{80,96},{96,112},{112,128},... | collective-permute-start | bytes 393224 | tf_op jit(solution)/shard_map/ppermute | solution.py:30
  200.9 7.0 %collective-permute-start.12 = (f32[8,10,1,256]{3,0,2,1:T(8,128)S(1)}, f32[8,10,1,256]{3,0,2,1:T(8,128)S(1)}, u32[]{:S(2)}, u32[]{:S(2)}) collective-permute-start(f32[8,10,1,256]{3,0,2,1:T(8,128)S(1)} %copy.435), channel_id=1, source_target_pairs={{1,0},{2,1},{3,2},{4,3},{5,4},{6,5},{7,6},{8,7},{9,8},{10,9},{11,1... | collective-permute-start | bytes 245768 | tf_op jit(solution)/shard_map/ppermute | solution.py:32
  203.9 4.1 collective-permute-start.13
  237.8 5.3 %collective-permute-start.16 = (f32[8,1,8,128]{3,2,1,0:T(8,128)S(1)}, f32[8,1,8,128]{3,2,1,0:T(8,128)S(1)}, u32[]{:S(2)}, u32[]{:S(2)}) collective-permute-start(f32[8,1,8,128]{3,2,1,0:T(8,128)S(1)} %get-tuple-element.59), channel_id=1, source_target_pairs={{16,0},{32,16},{48,32},{64,48},{80,64},{96,80},{112,96},{128,112},... | collective-permute-start | bytes 98312 | tf_op jit(solution)/shard_map/ppermute | solution.py:32
  239.1 5.0 %collective-permute-start.17 = (f32[8,1,8,128]{3,2,1,0:T(8,128)S(1)}, f32[8,1,8,128]{3,2,1,0:T(8,128)S(1)}, u32[]{:S(2)}, u32[]{:S(2)}) collective-permute-start(f32[8,1,8,128]{3,2,1,0:T(8,128)S(1)} %get-tuple-element.58), channel_id=1, source_target_pairs={{0,16},{16,32},{32,48},{48,64},{64,80},{80,96},{96,112},{112,128},... | collective-permute-start | bytes 98312 | tf_op jit(solution)/shard_map/ppermute | solution.py:30
  244.1 7.3 %collective-permute-start.18 = (f32[8,6,1,128]{3,2,1,0:T(1,128)S(1)}, f32[8,6,1,128]{3,2,1,0:T(1,128)S(1)}, u32[]{:S(2)}, u32[]{:S(2)}) collective-permute-start(f32[8,6,1,128]{3,2,1,0:T(1,128)S(1)} %get-tuple-element.52), channel_id=1, source_target_pairs={{1,0},{2,1},{3,2},{4,3},{5,4},{6,5},{7,6},{8,7},{9,8},{10,9},{11,1... | collective-permute-start | bytes 73736 | tf_op jit(solution)/shard_map/ppermute | solution.py:32
  247.0 5.3 %collective-permute-start.19 = (f32[8,6,1,128]{3,2,1,0:T(1,128)S(1)}, f32[8,6,1,128]{3,2,1,0:T(1,128)S(1)}, u32[]{:S(2)}, u32[]{:S(2)}) collective-permute-start(f32[8,6,1,128]{3,2,1,0:T(1,128)S(1)} %get-tuple-element.53), channel_id=1, source_target_pairs={{0,1},{1,2},{2,3},{3,4},{4,5},{5,6},{6,7},{7,8},{8,9},{9,10},{10,1... | collective-permute-start | bytes 73736 | tf_op jit(solution)/shard_map/ppermute | solution.py:30
  253.4 5.9 %collective-permute-start.20 = (f32[8,1,8,128]{3,2,1,0:T(8,128)S(1)}, f32[8,1,8,128]{3,2,1,0:T(8,128)S(1)}, u32[]{:S(2)}, u32[]{:S(2)}) collective-permute-start(f32[8,1,8,128]{3,2,1,0:T(8,128)S(1)} %get-tuple-element.57), channel_id=1, source_target_pairs={{16,0},{32,16},{48,32},{64,48},{80,64},{96,80},{112,96},{128,112},... | collective-permute-start | bytes 98312 | tf_op jit(solution)/shard_map/ppermute | solution.py:32
  254.7 5.6 %collective-permute-start.21 = (f32[8,1,8,128]{3,2,1,0:T(8,128)S(1)}, f32[8,1,8,128]{3,2,1,0:T(8,128)S(1)}, u32[]{:S(2)}, u32[]{:S(2)}) collective-permute-start(f32[8,1,8,128]{3,2,1,0:T(8,128)S(1)} %get-tuple-element.56), channel_id=1, source_target_pairs={{0,16},{16,32},{32,48},{48,64},{64,80},{80,96},{96,112},{112,128},... | collective-permute-start | bytes 98312 | tf_op jit(solution)/shard_map/ppermute | solution.py:30
  260.4 7.0 %collective-permute-start.22 = (f32[8,6,1,128]{3,2,1,0:T(1,128)S(1)}, f32[8,6,1,128]{3,2,1,0:T(1,128)S(1)}, u32[]{:S(2)}, u32[]{:S(2)}) collective-permute-start(f32[8,6,1,128]{3,2,1,0:T(1,128)S(1)} %get-tuple-element.50), channel_id=1, source_target_pairs={{1,0},{2,1},{3,2},{4,3},{5,4},{6,5},{7,6},{8,7},{9,8},{10,9},{11,1... | collective-permute-start | bytes 73736 | tf_op jit(solution)/shard_map/ppermute | solution.py:32
  262.3 6.0 %collective-permute-start.23 = (f32[8,6,1,128]{3,2,1,0:T(1,128)S(1)}, f32[8,6,1,128]{3,2,1,0:T(1,128)S(1)}, u32[]{:S(2)}, u32[]{:S(2)}) collective-permute-start(f32[8,6,1,128]{3,2,1,0:T(1,128)S(1)} %get-tuple-element.51), channel_id=1, source_target_pairs={{0,1},{1,2},{2,3},{3,4},{4,5},{5,6},{6,7},{7,8},{8,9},{9,10},{10,1... | collective-permute-start | bytes 73736 | tf_op jit(solution)/shard_map/ppermute | solution.py:30
  268.5 5.9 %collective-permute-start.24 = (f32[8,1,8,128]{3,2,1,0:T(8,128)S(1)}, f32[8,1,8,128]{3,2,1,0:T(8,128)S(1)}, u32[]{:S(2)}, u32[]{:S(2)}) collective-permute-start(f32[8,1,8,128]{3,2,1,0:T(8,128)S(1)} %get-tuple-element.55), channel_id=1, source_target_pairs={{16,0},{32,16},{48,32},{64,48},{80,64},{96,80},{112,96},{128,112},... | collective-permute-start | bytes 98312 | tf_op jit(solution)/shard_map/ppermute | solution.py:32
  269.8 5.6 %collective-permute-start.25 = (f32[8,1,8,128]{3,2,1,0:T(8,128)S(1)}, f32[8,1,8,128]{3,2,1,0:T(8,128)S(1)}, u32[]{:S(2)}, u32[]{:S(2)}) collective-permute-start(f32[8,1,8,128]{3,2,1,0:T(8,128)S(1)} %get-tuple-element.54), channel_id=1, source_target_pairs={{0,16},{16,32},{32,48},{48,64},{64,80},{80,96},{96,112},{112,128},... | collective-permute-start | bytes 98312 | tf_op jit(solution)/shard_map/ppermute | solution.py:30
  275.4 7.0 %collective-permute-start.26 = (f32[8,6,1,128]{3,2,1,0:T(1,128)S(1)}, f32[8,6,1,128]{3,2,1,0:T(1,128)S(1)}, u32[]{:S(2)}, u32[]{:S(2)}) collective-permute-start(f32[8,6,1,128]{3,2,1,0:T(1,128)S(1)} %get-tuple-element.48), channel_id=1, source_target_pairs={{1,0},{2,1},{3,2},{4,3},{5,4},{6,5},{7,6},{8,7},{9,8},{10,9},{11,1... | collective-permute-start | bytes 73736 | tf_op jit(solution)/shard_map/ppermute | solution.py:32
  277.4 6.0 %collective-permute-start.27 = (f32[8,6,1,128]{3,2,1,0:T(1,128)S(1)}, f32[8,6,1,128]{3,2,1,0:T(1,128)S(1)}, u32[]{:S(2)}, u32[]{:S(2)}) collective-permute-start(f32[8,6,1,128]{3,2,1,0:T(1,128)S(1)} %get-tuple-element.49), channel_id=1, source_target_pairs={{0,1},{1,2},{2,3},{3,4},{4,5},{5,6},{6,7},{7,8},{8,9},{9,10},{10,1... | collective-permute-start | bytes 73736 | tf_op jit(solution)/shard_map/ppermute | solution.py:30
  306.3 6.5 %collective-permute-start.28 = (f32[8,1,16,256]{3,2,1,0:T(8,128)S(1)}, f32[8,1,16,256]{3,2,1,0:T(8,128)S(1)}, u32[]{:S(2)}, u32[]{:S(2)}) collective-permute-start(f32[8,1,16,256]{3,2,1,0:T(8,128)S(1)} %get-tuple-element.41), channel_id=1, source_target_pairs={{16,0},{32,16},{48,32},{64,48},{80,64},{96,80},{112,96},{128,112},... | collective-permute-start | bytes 393224 | tf_op jit(solution)/shard_map/ppermute | solution.py:32
  307.7 6.5 %collective-permute-start.29 = (f32[8,1,16,256]{3,2,1,0:T(8,128)S(1)}, f32[8,1,16,256]{3,2,1,0:T(8,128)S(1)}, u32[]{:S(2)}, u32[]{:S(2)}) collective-permute-start(f32[8,1,16,256]{3,2,1,0:T(8,128)S(1)} %get-tuple-element.40), channel_id=1, source_target_pairs={{0,16},{16,32},{32,48},{48,64},{64,80},{80,96},{96,112},{112,128},... | collective-permute-start | bytes 393224 | tf_op jit(solution)/shard_map/ppermute | solution.py:30
  314.4 7.2 %collective-permute-start.30 = (f32[8,10,1,256]{3,0,2,1:T(8,128)S(1)}, f32[8,10,1,256]{3,0,2,1:T(8,128)S(1)}, u32[]{:S(2)}, u32[]{:S(2)}) collective-permute-start(f32[8,10,1,256]{3,0,2,1:T(8,128)S(1)} %copy.446), channel_id=1, source_target_pairs={{1,0},{2,1},{3,2},{4,3},{5,4},{6,5},{7,6},{8,7},{9,8},{10,9},{11,1... | collective-permute-start | bytes 245768 | tf_op jit(solution)/shard_map/ppermute | solution.py:32
  316.3 6.5 %collective-permute-start.31 = (f32[8,10,1,256]{3,0,2,1:T(8,128)S(1)}, f32[8,10,1,256]{3,0,2,1:T(8,128)S(1)}, u32[]{:S(2)}, u32[]{:S(2)}) collective-permute-start(f32[8,10,1,256]{3,0,2,1:T(8,128)S(1)} %copy.448), channel_id=1, source_target_pairs={{0,1},{1,2},{2,3},{3,4},{4,5},{5,6},{6,7},{7,8},{8,9},{9,10},{10,1... | collective-permute-start | bytes 245768 | tf_op jit(solution)/shard_map/ppermute | solution.py:30
  (37 other events, 579.5 us)
